TPU v7x, 256 devices: a whole 4x4x8 slice. The times are simulated.
256 devices in a mesh: row: 32 (over x, y, core), col: 8 (over z).
Axes of the slice: x: 4, y: 4, z: 8, core: 2. Of those that a mesh axis runs over, the one named last changes fastest.
Arguments:
- inputs: float32 [512, 12288], P('row', 'col'), may hold values from -600 to 600, as said below
- gain: float32 [12288], P('col'), may hold values from 0.1 to 1.9
- bias: float32 [12288], P('col'), may hold values from -3 to 3
- weight: bfloat16 [12288, 49152], P('col', 'row'), may hold values from -0.0546875 to 0.0546875
- d_act: bfloat16 [512, 49152], P('col', 'row'), may hold values from -1.5 to 1.5
Outputs:
- activated: bfloat16 [512, 49152], P('col', 'row')
- d_normed: bfloat16 [512, 12288], P('row', 'col')
- d_weight: bfloat16 [12288, 49152], P('col', 'row')
Inputs may be any that keep to these rules, and one draw needn't show every extreme that they name: `inputs`: finite values.
All inputs are finite; a program needn't handle non-finite values.
Results may differ from a plain program's by a relative error of at most 0.024.
Values may be sent and summed in bfloat16 or wider, within the bound.
No kernel may reach another device: no remote copies, remote signals or barrier semaphores. Data moves between devices by JAX's collectives and lax.ppermute only.
A program may use at most 64 MiB of HBM per device.

v0:
```python
import jax
import jax.numpy as jnp
from jax import lax
from jax.sharding import PartitionSpec as P

D = 12288


def gelu_tanh(value):
    return jax.nn.gelu(value, approximate=True)


def per_device(inputs, gain, bias, weight, d_act):
    row_mean = lax.psum(jnp.sum(inputs, axis=1, keepdims=True), "col") / D
    centered = inputs - row_mean
    spread = lax.psum(jnp.sum(centered * centered, axis=1, keepdims=True), "col") / D
    normed = (centered * lax.rsqrt(spread + 1e-05) * gain[None, :] + bias[None, :]).astype(
        jnp.bfloat16
    )
    gathered = lax.all_gather(normed, "row", axis=0, tiled=True)
    block_rows = gathered
    pre = lax.psum_scatter(
        jnp.dot(block_rows, weight, preferred_element_type=jnp.float32).astype(jnp.bfloat16),
        "col",
        scatter_dimension=0,
        tiled=True,
    ).astype(jnp.float32)
    result, pullback = jax.vjp(gelu_tanh, pre)
    activated = result.astype(jnp.bfloat16)
    d_pre = pullback(d_act.astype(jnp.float32))[0].astype(jnp.bfloat16)
    slopes = lax.all_gather(d_pre, "col", axis=0, tiled=True)
    d_weight = lax.dot_general(
        gathered, slopes, (((0,), (0,)), ((), ())), preferred_element_type=jnp.float32
    ).astype(jnp.bfloat16)
    block_rows = slopes
    d_normed = lax.psum_scatter(
        lax.dot_general(
            block_rows, weight, (((1,), (1,)), ((), ())), preferred_element_type=jnp.float32
        ).astype(jnp.bfloat16),
        "row",
        scatter_dimension=0,
        tiled=True,
    )
    return (activated, d_normed, d_weight)


def solution(mesh):
    return jax.shard_map(
        per_device,
        mesh=mesh,
        in_specs=(P("row", "col"), P("col"), P("col"), P("col", "row"), P("col", "row")),
        out_specs=(P("col", "row"), P("row", "col"), P("col", "row")),
        check_vma=False,
    )
```

profile of v0, /device:TPU:2, one launch (start us, length us, event | category | flops | bytes accessed | tf_op | source)
XLA Modules:
  0.0 277.8 jit_solution(4469561945368049492)
XLA Ops:
  7.2 0.0 all-gather.3.cloned.1.call-start
  7.2 1.0 reduce_sum.18
  8.2 20.0 %psum.14 = f32[16,1]{0,1:T(1,128)S(1)} all-reduce(f32[16,1]{0,1:T(1,128)S(1)} %bitcast.12), channel_id=1, replica_groups=mesh['row'=32,'col'=8] {'col'}, use_global_device_ids=true, to_apply=%region_1.0 | all-reduce | flops 16 | bytes 128 | tf_op jit(solution)/shard_map/psum | solution.py:14
  28.2 1.1 multiply_reduce_fusion
  29.3 14.2 %psum.15 = f32[16,1]{0,1:T(1,128)S(1)} all-reduce(f32[16,1]{0,1:T(1,128)S(1)} %bitcast.13), channel_id=1, replica_groups=mesh['row'=32,'col'=8] {'col'}, use_global_device_ids=true, to_apply=%region_3.0 | all-reduce | flops 16 | bytes 128 | tf_op jit(solution)/shard_map/psum | solution.py:16
  43.5 1.6 add_convert_fusion
  45.1 0.0 all-gather.3.cloned.1.call-update
  45.1 0.0 reduce-scatter.3.cloned.1.call-start
  45.2 47.2 %all-gather.3.cloned.1.call-done = bf16[512,1536]{1,0:T(8,128)(2,1)} async-done(((bf16[16,1536]{1,0:T(8,128)(2,1)}), bf16[512,1536]{1,0:T(8,128)(2,1)}) %all-gather.3.cloned.1.call-update) | async-done | bytes 1572880 | tf_op jit(solution)/shard_map/all_gather | solution.py:20
  92.4 6.6 %convolution_convert_fusion.2 = bf16[512,1536]{1,0:T(8,128)(2,1)} fusion(bf16[512,1536]{1,0:T(8,128)(2,1)} %all-gather.3.cloned.1.call-done, bf16[1536,1536]{1,0:T(8,128)(2,1)} %param.8), kind=kOutput, calls=%fused_computation.2 | convolution fusion | flops 2416705536 | bytes 7864320 | tf_op jit(solution)/shard_map/dot_general | solution.py:23
  98.9 0.0 copy-start
  98.9 0.0 reduce-scatter.3.cloned.1.call-update
  98.9 0.0 all-gather.5.cloned.1.call-start
  99.0 40.3 %reduce-scatter.3.cloned.1.call-done = bf16[64,1536]{1,0:T(8,128)(2,1)} async-done(((bf16[512,1536]{1,0:T(8,128)(2,1)}), bf16[64,1536]{1,0:T(8,128)(2,1)}) %reduce-scatter.3.cloned.1.call-update) | async-done | bytes 196624 | tf_op jit(solution)/shard_map/reduce_scatter | solution.py:22
  139.3 0.0 copy-done
  139.3 2.0 fusion.3
  141.3 0.0 all-gather.5.cloned.1.call-update
  141.3 0.0 reduce-scatter.5.cloned.1.call-start
  141.3 38.8 %all-gather.5.cloned.1.call-done = bf16[512,1536]{1,0:T(8,128)(2,1)} async-done(((bf16[64,1536]{1,0:T(8,128)(2,1)}), bf16[512,1536]{1,0:T(8,128)(2,1)}) %all-gather.5.cloned.1.call-update) | async-done | bytes 1572880 | tf_op jit(solution)/shard_map/all_gather | solution.py:31
  180.2 0.0 copy-start.2
  180.2 6.7 %convolution_convert_fusion.1 = bf16[512,1536]{1,0:T(8,128)(2,1)} fusion(bf16[512,1536]{1,0:T(8,128)(2,1)} %all-gather.5.cloned.1.call-done, bf16[1536,1536]{1,0:T(8,128)(2,1)} %param.8), kind=kOutput, calls=%fused_computation.1 | convolution fusion | flops 2416705536 | bytes 7864320 | tf_op jit(solution)/shard_map/dot_general | solution.py:37
  186.9 0.0 copy-start.1
  186.9 0.0 reduce-scatter.5.cloned.1.call-update
  186.9 0.0 copy-done.2
  186.9 1.4 copy-done.1
  188.3 4.3 %convolution_convert_fusion = bf16[1536,1536]{1,0:T(8,128)(2,1)} fusion(bf16[512,1536]{1,0:T(8,128)(2,1)S(1)} %copy-done.1, bf16[512,1536]{1,0:T(8,128)(2,1)S(1)} %copy-done.2), kind=kOutput, calls=%fused_computation | convolution fusion | flops 2418278400 | bytes 7864320 | tf_op jit(solution)/shard_map/dot_general | solution.py:32
  192.6 78.7 %reduce-scatter.5.cloned.1.call-done = bf16[16,1536]{1,0:T(8,128)(2,1)} async-done(((bf16[512,1536]{1,0:T(8,128)(2,1)}), bf16[16,1536]{1,0:T(8,128)(2,1)}) %reduce-scatter.5.cloned.1.call-update) | async-done | bytes 49168 | tf_op jit(solution)/shard_map/reduce_scatter | solution.py:36
  (2 shorter events, 0.0 us)
Async XLA Ops:
  7.2 85.2 %all-gather.3.cloned.1.call-start = ((), (), s32[]{:S(2)}) async-start(), calls=%async_computation.2 | async-start | bytes 1622016 | tf_op jit(solution)/shard_map/all_gather | solution.py:20
  45.1 94.2 %reduce-scatter.3.cloned.1.call-start = ((), (), s32[]{:S(2)}) async-start(), calls=%async_computation.3 | async-start | bytes 1769472 | tf_op jit(solution)/shard_map/reduce_scatter | solution.py:22
  98.9 40.4 %copy-start = (bf16[64,1536]{1,0:T(8,128)(2,1)S(1)}, bf16[64,1536]{1,0:T(8,128)(2,1)}, u32[]{:S(2)}) copy-start(bf16[64,1536]{1,0:T(8,128)(2,1)} %param.9) | copy-start | bytes 589828
  98.9 81.2 %all-gather.5.cloned.1.call-start = ((), (), s32[]{:S(2)}) async-start(), calls=%async_computation.4 | async-start | bytes 1769472 | tf_op jit(solution)/shard_map/all_gather | solution.py:31
  141.3 129.9 %reduce-scatter.5.cloned.1.call-start = ((), (), s32[]{:S(2)}) async-start(), calls=%async_computation.5 | async-start | bytes 1622016 | tf_op jit(solution)/shard_map/reduce_scatter | solution.py:36
  180.2 6.7 %copy-start.2 = (bf16[512,1536]{1,0:T(8,128)(2,1)S(1)}, bf16[512,1536]{1,0:T(8,128)(2,1)}, u32[]{:S(2)}) copy-start(bf16[512,1536]{1,0:T(8,128)(2,1)} %all-gather.5.cloned.1.call-done) | copy-start | bytes 4718596
  186.9 1.4 copy-start.1
Sparse Core Ops, SparseCore 0:
  45.2 47.0 all-gather.2
  99.1 40.1 reduce-scatter.2
  141.7 38.4 all-gather.4
  187.0 84.1 reduce-scatter.4
where the time goes:
time: 278 us
  waiting for transfers between devices  205 us (74%)
  blocking collectives  34.2 us (12%)
  matrix products  17.5 us (6%)
  between operations  13.8 us (5%)
  other arithmetic  5.72 us (2%)
    reduce_scatter x1, waiting for transfers between devices, per_device(): lax.psum_scatter(lax.dot_general(block_rows, weight, (((1,), (1,)), ((),...  78.7 us
    all_gather x1, waiting for transfers between devices, per_device(): gathered = lax.all_gather(normed, 'row', axis=0, tiled=True)  47.2 us
    reduce_scatter x1, waiting for transfers between devices, per_device(): lax.psum_scatter(jnp.dot(block_rows, weight, preferred_element_type=jnp.f...  40.3 us
    all_gather x1, waiting for transfers between devices, per_device(): slopes = lax.all_gather(d_pre, 'col', axis=0, tiled=True)  38.8 us
    psum x1, blocking collectives, per_device(): row_mean = lax.psum(jnp.sum(inputs, axis=1, keepdims=True), 'col') / D  20 us
    psum x1, blocking collectives, per_device(): lax.psum(jnp.sum(centered * centered, axis=1, keepdims=True), 'col') / D  14.2 us
    dot_general x1, matrix products, per_device(): lax.dot_general(block_rows, weight, (((1,), (1,)), ((), ())), preferred_e...  6.7 us
    dot_general x1, matrix products, per_device(): jnp.dot(block_rows, weight, preferred_element_type=jnp.float32)  6.56 us
  transfers between devices with their start and end apart: 4, of which 4 were waited for; matrix products, arithmetic and copies ran while one was open for 2% of the time, Pallas kernels for 0%

commit v1 on v0

v1 whole, which is shorter than its diff:
```python
import functools

import jax
import jax.numpy as jnp
from jax import lax
from jax.experimental import pallas as pl
from jax.experimental.pallas import tpu as pltpu
from jax.sharding import Mesh
from jax.sharding import PartitionSpec as P

D = 12288
F32, BF16 = jnp.float32, jnp.bfloat16

NX, NY, NC, NZ = 4, 4, 2, 8
CHIPS = NX * NY
OWN = 16
TOKENS_Z = 64
TOKENS = 512
BACKWARD = [list(range(NZ))[::-1]]

VMEM = pl.BlockSpec(memory_space=pltpu.VMEM)
HBM = pl.BlockSpec(memory_space=pltpu.HBM)


def fetch(source, held, sems, steps, piece):
    copies = [
        pltpu.make_async_copy(source.at[piece(i)], held.at[i], sems.at[i]) for i in range(steps)
    ]
    for copy in copies:
        copy.start()
    return copies


def token_offset(chip, core_shift):
    core = (lax.axis_index("core") + core_shift) % NC
    return pl.multiple_of((chip * NC + core) * OWN, OWN)


def z_rows(k, reverse):
    k = NZ - 1 - k if reverse else k
    return slice(k * TOKENS_Z, (k + 1) * TOKENS_Z)


def multiply(steps, tile, copies, normed_ref, held, out_ref, reverse):
    for i in range(steps):
        copies[i].wait()
        product = jnp.dot(normed_ref[...], held[i], preferred_element_type=F32).astype(BF16)
        for k in range(NZ):
            out_ref[z_rows(k, reverse), i * tile : (i + 1) * tile] = product[z_rows(k, False), :]


def first_kernel(steps, tile, base, own_ref, other_ref, w_ref, normed_ref, out_ref, held, sems):
    copies = fetch(w_ref, held, sems, steps, lambda i: (slice(None), pl.ds(base + i * tile, tile)))
    for core_shift, piece in enumerate((own_ref, other_ref)):
        for chip in range(CHIPS):
            normed_ref[pl.ds(token_offset(chip, core_shift), OWN), :] = piece[
                chip * OWN : (chip + 1) * OWN, :
            ]
    multiply(steps, tile, copies, normed_ref, held, out_ref, False)


def second_kernel(steps, tile, base, normed_ref, w_ref, out_ref, held, sems):
    copies = fetch(w_ref, held, sems, steps, lambda i: (slice(None), pl.ds(base + i * tile, tile)))
    multiply(steps, tile, copies, normed_ref, held, out_ref, True)


def partial_pre(kernel, operands, weight, half, tile, first):
    depth, width = weight.shape
    steps = width // 2 // tile
    outs = [jax.ShapeDtypeStruct((TOKENS, width // 2), BF16)]
    if first:
        outs = [jax.ShapeDtypeStruct((TOKENS, depth), BF16)] + outs
    return pl.pallas_call(
        functools.partial(kernel, steps, tile, half * width // 2),
        in_specs=[VMEM] * len(operands) + [HBM],
        out_specs=[VMEM] * len(outs),
        out_shape=outs,
        scratch_shapes=[pltpu.VMEM((steps, depth, tile), BF16), pltpu.SemaphoreType.DMA((steps,))],
        compiler_params=pltpu.CompilerParams(vmem_limit_bytes=24 << 20),
        cost_estimate=pl.CostEstimate(
            flops=TOKENS * depth * width, bytes_accessed=depth * width * 2, transcendentals=0
        ),
    )(*operands, weight)


def third_kernel(steps, tile, a_ref, b_ref, w_ref, slopes_ref, own_ref, other_ref, held, acc, sems):
    half = slopes_ref.shape[1] // 2
    copies = fetch(w_ref, held, sems, steps, lambda i: (pl.ds(i * tile, tile), slice(None)))
    slopes_ref[:, :half] = a_ref[...]
    for k in range(NZ):
        slopes_ref[z_rows(k, False), half:] = b_ref[z_rows(k, True), :]
    for step in range(steps):
        copies[step].wait()
        acc[...] = lax.dot_general(
            slopes_ref[...], held[step], (((1,), (1,)), ((), ())), preferred_element_type=F32
        )
        columns = slice(step * tile, (step + 1) * tile)
        for core_shift, piece in enumerate((own_ref, other_ref)):
            for chip in range(CHIPS):
                piece[chip * OWN : (chip + 1) * OWN, columns] = acc[
                    pl.ds(token_offset(chip, core_shift), OWN), :
                ].astype(BF16)


def partial_normed(slopes_a, slopes_b, weight, tile):
    depth, width = weight.shape
    steps = depth // tile
    return pl.pallas_call(
        functools.partial(third_kernel, steps, tile),
        in_specs=[VMEM, VMEM, HBM],
        out_specs=[VMEM] * 3,
        out_shape=[
            jax.ShapeDtypeStruct((TOKENS, width), BF16),
            jax.ShapeDtypeStruct((TOKENS // 2, depth), BF16),
            jax.ShapeDtypeStruct((TOKENS // 2, depth), BF16),
        ],
        scratch_shapes=[
            pltpu.VMEM((steps, tile, width), BF16),
            pltpu.VMEM((TOKENS, tile), F32),
            pltpu.SemaphoreType.DMA((steps,)),
        ],
        compiler_params=pltpu.CompilerParams(vmem_limit_bytes=24 << 20),
        cost_estimate=pl.CostEstimate(
            flops=2 * TOKENS * depth * width, bytes_accessed=depth * width * 2, transcendentals=0
        ),
    )(slopes_a, slopes_b, weight)


def gelu_tanh(value):
    return jax.nn.gelu(value, approximate=True)


def send_core(value):
    return lax.ppermute(value, "core", [(0, 1), (1, 0)])


def normalize(inputs, gain, bias):
    local = inputs.shape[1]
    local_mean = jnp.sum(inputs, axis=1) / local
    centered = inputs - local_mean[:, None]
    local_square = jnp.sum(centered * centered, axis=1)
    stats = jnp.stack([local_mean, local_square])
    every = lax.all_to_all(jnp.broadcast_to(stats[None], (NZ,) + stats.shape), "col", 0, 0)
    mean = jnp.mean(every[:, 0, :], axis=0)
    offset = every[:, 0, :] - mean[None, :]
    spread = (jnp.sum(every[:, 1, :], axis=0) + local * jnp.sum(offset * offset, axis=0)) / D
    scale = lax.rsqrt(spread + 1e-05)
    moved = centered + (local_mean - mean)[:, None]
    return (moved * scale[:, None] * gain[None, :] + bias[None, :]).astype(BF16)


def per_device(inputs, gain, bias, weight, d_act):
    half = weight.shape[1] // 2
    depth = weight.shape[0]
    normed = normalize(inputs, gain, bias)

    copies = jnp.broadcast_to(normed[None], (CHIPS, OWN, depth))
    plane = lax.all_to_all(copies, ("x", "y"), 0, 0).reshape(CHIPS * OWN, depth)
    other = send_core(plane)

    gathered, part_a = partial_pre(first_kernel, [plane, other], weight, 0, 256, True)
    (part_b,) = partial_pre(second_kernel, [gathered], weight, 1, 256, False)
    total_a = lax.psum_scatter(part_a, "col", scatter_dimension=0, tiled=True)
    total_b = lax.psum_scatter(
        part_b, "col", scatter_dimension=0, tiled=True, axis_index_groups=BACKWARD
    )

    activated, slopes = [], []
    for h, total in enumerate((total_a, total_b)):
        result, pullback = jax.vjp(gelu_tanh, total.astype(F32))
        activated.append(result.astype(BF16))
        cotangent = d_act[:, h * half : (h + 1) * half].astype(F32)
        slopes.append(pullback(cotangent)[0].astype(BF16))
    slopes_a = lax.all_gather(slopes[0], "col", axis=0, tiled=True)
    slopes_b = lax.all_gather(
        slopes[1], "col", axis=0, tiled=True, axis_index_groups=BACKWARD
    )

    slopes_all, own, other = partial_normed(slopes_a, slopes_b, weight, 256)
    d_weight = lax.dot_general(
        gathered, slopes_all, (((0,), (0,)), ((), ())), preferred_element_type=F32
    ).astype(BF16)

    chip_sum = (own.astype(F32) + send_core(other).astype(F32)).astype(BF16)
    arrived = lax.all_to_all(chip_sum.reshape(CHIPS, OWN, depth), ("x", "y"), 0, 0)
    d_normed = jnp.sum(arrived.astype(F32), axis=0).astype(BF16)
    return (jnp.concatenate(activated, axis=1), d_normed, d_weight)


def solution(mesh):
    split = Mesh(mesh.devices.reshape(NX, NY, NC, NZ), ("x", "y", "core", "col"))
    row = ("x", "y", "core")
    return jax.shard_map(
        per_device,
        mesh=split,
        in_specs=(P(row, "col"), P("col"), P("col"), P("col", row), P("col", row)),
        out_specs=(P("col", row), P(row, "col"), P("col", row)),
        check_vma=False,
    )
```

time: 278 us -> 221 us (0.79)
  waiting for transfers between devices: 205 us -> 77.8 us
  blocking collectives: 34.2 us -> 86.7 us
  Pallas kernels: 0 us -> 13.8 us
  matrix products: 17.5 us -> 4.27 us
  starting transfers between devices: 0.16 us -> 7.46 us
  local copies, waits for them, and re-layouts: 1.38 us -> 7.09 us
    all_gather x2 -> x0, waiting for transfers between devices: 86 us -> none  [the longest x1 47.2 us: per_device(): gathered = lax.all_gather(normed, 'row', axis=0, tiled=True)]
    reduce_scatter x2, waiting for transfers between devices: 119 us -> 65.7 us  [the longest x1 39.2 us: per_device(): lax.psum_scatter(part_b, 'col', scatter_dimension=0, tiled=True, axis_ind...]
    all_gather x0 -> x2, blocking collectives: none -> 52.4 us  [the longest x1 26.3 us: per_device(): lax.all_gather(slopes[1], 'col', axis=0, tiled=True, axis_index_groups=BA...]
    all_to_all x0 -> x2, blocking collectives: none -> 34.2 us  [the longest x1 18.3 us: per_device(): plane = lax.all_to_all(copies, ('x', 'y'), 0, 0).reshape(CHIPS * OWN, depth)]
    psum x2 -> x0, blocking collectives: 34.2 us -> none  [the longest x1 20 us: per_device(): row_mean = lax.psum(jnp.sum(inputs, axis=1, keepdims=True), 'col') / D]
    pallas_call x0 -> x3, Pallas kernels: none -> 13.8 us  [the longest x2 7.23 us: partial_pre(): pl.pallas_call(functools.partial(kernel, steps, tile, half * width // 2),...]
    dot_general x3 -> x1, matrix products: 17.5 us -> 4.27 us  [per_device(): lax.dot_general(gathered, slopes_all, (((0,), (0,)), ((), ())), preferred...]
    all_to_all x0 -> x1, waiting for transfers between devices: none -> 7.52 us  [per_device(): lax.all_to_all(chip_sum.reshape(CHIPS, OWN, depth), ('x', 'y'), 0, 0)]
  transfers between devices with their start and end apart: 4 -> 5, of which waited for: 4 -> 5; matrix products, arithmetic and copies ran while one was open for 2% -> 2% of each run, Pallas kernels for 0% -> 2%
where the time goes in v1:
time: 221 us; the launch traced here: 219 us
  blocking collectives  86.7 us (39%)
  waiting for transfers between devices  77.8 us (35%)
  between operations  14.1 us (6%)
  Pallas kernels  13.8 us (6%)
  other arithmetic  8.12 us (4%)
  starting transfers between devices  7.46 us (3%)
  local copies, waits for them, and re-layouts  7.09 us (3%)
  matrix products  4.27 us (2%)
    reduce_scatter x1, waiting for transfers between devices, per_device(): lax.psum_scatter(part_b, 'col', scatter_dimension=0, tiled=True, axis_ind...  39.2 us
    reduce_scatter x1, waiting for transfers between devices, per_device(): total_a = lax.psum_scatter(part_a, 'col', scatter_dimension=0, tiled=True)  26.5 us
    all_gather x1, blocking collectives, per_device(): lax.all_gather(slopes[1], 'col', axis=0, tiled=True, axis_index_groups=BA...  26.3 us
    all_gather x1, blocking collectives, per_device(): slopes_a = lax.all_gather(slopes[0], 'col', axis=0, tiled=True)  26.1 us
    all_to_all x1, blocking collectives, per_device(): plane = lax.all_to_all(copies, ('x', 'y'), 0, 0).reshape(CHIPS * OWN, depth)  18.3 us
    all_to_all x1, blocking collectives, normalize(): lax.all_to_all(jnp.broadcast_to(stats[None], (NZ,) + stats.shape), 'col',...  16 us
    all_to_all x1, waiting for transfers between devices, per_device(): lax.all_to_all(chip_sum.reshape(CHIPS, OWN, depth), ('x', 'y'), 0, 0)  7.52 us
    all_to_all x1, starting transfers between devices, per_device(): lax.all_to_all(chip_sum.reshape(CHIPS, OWN, depth), ('x', 'y'), 0, 0)  7.28 us
  transfers between devices with their start and end apart: 5, of which 5 were waited for; matrix products, arithmetic and copies ran while one was open for 2% of the time, Pallas kernels for 2%

profile of v1, /device:TPU:2, one launch (start us, length us, event | category | flops | bytes accessed | tf_op | source)
XLA Modules:
  0.0 219.4 jit_solution(11114156787420993492)
XLA Ops:
  7.2 0.0 reduce-scatter.3.cloned.1.call-start
  7.2 1.0 reduce_sum.57
  8.2 1.1 multiply_reduce_fusion
  9.3 16.0 %all_to_all.15 = f32[8,2,16]{2,1,0:T(2,128)S(1)} all-to-all(f32[8,2,16]{2,1,0:T(2,128)S(1)} %broadcast_in_dim.4), channel_id=1, replica_groups=mesh['x'=4,'y'=4,'core'=2,'col'=8] {'col'}, dimensions={0} | all-to-all | bytes 2048 | tf_op jit(solution)/shard_map/all_to_all | solution.py:143
  25.4 1.0 add_convert_fusion.1
  26.4 0.1 broadcast_in_dim.5
  26.5 18.3 %all_to_all.16 = bf16[16,16,1536]{2,1,0:T(8,128)(2,1)S(1)} all-to-all(bf16[16,16,1536]{2,1,0:T(8,128)(2,1)S(1)} %broadcast_in_dim.5), channel_id=1, replica_groups=mesh['x'=4,'y'=4,'core'=2,'col'=8] {'x','y'}, dimensions={0} | all-to-all | bytes 1572864 | tf_op jit(solution)/shard_map/all_to_all | solution.py:158
  44.8 0.0 collective-permute-start
  44.8 2.3 %collective-permute-done.other_ref = bf16[256,1536]{1,0:T(8,128)(2,1)S(1)} collective-permute-done((bf16[256,1536]{1,0:T(8,128)(2,1)S(1)}, bf16[256,1536]{1,0:T(8,128)(2,1)S(1)}, u32[]{:S(2)}, u32[]{:S(2)}) %collective-permute-start) | collective-permute-done | bytes 786464 | tf_op jit(solution)/shard_map/ppermute | solution.py:134
  47.0 0.0 copy-start
  47.0 2.3 %copy-done = bf16[1536,1536]{1,0:T(8,128)(2,1)S(1)} copy-done((bf16[1536,1536]{1,0:T(8,128)(2,1)S(1)}, bf16[1536,1536]{1,0:T(8,128)(2,1)}, u32[]{:S(2)}) %copy-start) | copy-done | bytes 4718616
  49.4 3.7 %shard_map.76 = (bf16[512,1536]{1,0:T(8,128)(2,1)S(1)}, bf16[512,768]{1,0:T(8,128)(2,1)}) custom-call(bf16[256,1536]{1,0:T(8,128)(2,1)S(1)} %bitcast.11, bf16[256,1536]{1,0:T(8,128)(2,1)S(1)} %collective-permute-done.other_ref, bf16[1536,1536]{1,0:T(8,128)(2,1)S(1)} %copy-done), custom_call_target="tpu_custom_call" | custom-call | flops 1207959552 | bytes 4718592 | tf_op jit(solution)/shard_map/pallas_call | solution.py:73
  53.1 0.0 reduce-scatter.3.cloned.1.call-update
  53.1 0.0 reduce-scatter.5.cloned.1.call-start
  53.1 0.0 copy-start.1
  53.1 2.3 %copy-done.1 = bf16[1536,1536]{1,0:T(8,128)(2,1)S(1)} copy-done((bf16[1536,1536]{1,0:T(8,128)(2,1)S(1)}, bf16[1536,1536]{1,0:T(8,128)(2,1)}, u32[]{:S(2)}) %copy-start.1) | copy-done | bytes 4718616
  55.5 0.0 copy-start.3
  55.5 3.6 %shard_map.77 = bf16[512,768]{1,0:T(8,128)(2,1)} custom-call(bf16[512,1536]{1,0:T(8,128)(2,1)S(1)} %get-tuple-element.9.normed_ref, bf16[1536,1536]{1,0:T(8,128)(2,1)S(1)} %copy-done.1), custom_call_target="tpu_custom_call" | custom-call | flops 1207959552 | bytes 4718592 | tf_op jit(solution)/shard_map/pallas_call | solution.py:73
  59.0 0.0 reduce-scatter.5.cloned.1.call-update
  59.1 26.5 %reduce-scatter.3.cloned.1.call-done = bf16[64,768]{1,0:T(8,128)(2,1)} async-done(((bf16[512,768]{1,0:T(8,128)(2,1)}), bf16[64,768]{1,0:T(8,128)(2,1)}) %reduce-scatter.3.cloned.1.call-update) | async-done | bytes 98320 | tf_op jit(solution)/shard_map/reduce_scatter | solution.py:163
  85.6 39.2 %reduce-scatter.5.cloned.1.call-done = bf16[64,768]{1,0:T(8,128)(2,1)} async-done(((bf16[512,768]{1,0:T(8,128)(2,1)}), bf16[64,768]{1,0:T(8,128)(2,1)}) %reduce-scatter.5.cloned.1.call-update) | async-done | bytes 98320 | tf_op jit(solution)/shard_map/reduce_scatter | solution.py:164
  124.8 0.0 copy-done.3
  124.8 1.3 fusion.7
  126.0 26.3 %all_gather.7.b_ref = bf16[512,768]{1,0:T(8,128)(2,1)S(1)} all-gather(bf16[64,768]{1,0:T(8,128)(2,1)S(1)} %get-tuple-element.13), channel_id=1, replica_groups={{7,6,5,4,3,2,1,0},{15,14,13,12,11,10,9,8},{23,22,21,20,19,18,17,16},{31..., dimensions={0}, use_global_device_ids=true | all-gather | bytes 884736 | tf_op jit(solution)/shard_map/all_gather | solution.py:175
  152.4 26.1 %all_gather.6.a_ref = bf16[512,768]{1,0:T(8,128)(2,1)S(1)} all-gather(bf16[64,768]{1,0:T(8,128)(2,1)S(1)} %get-tuple-element.14), channel_id=1, replica_groups=mesh['x'=4,'y'=4,'core'=2,'col'=8] {'col'}, dimensions={0}, use_global_device_ids=true | all-gather | bytes 884736 | tf_op jit(solution)/shard_map/all_gather | solution.py:174
  178.5 0.0 copy-start.2
  178.5 2.3 %copy-done.2 = bf16[1536,1536]{1,0:T(8,128)(2,1)S(1)} copy-done((bf16[1536,1536]{1,0:T(8,128)(2,1)S(1)}, bf16[1536,1536]{1,0:T(8,128)(2,1)}, u32[]{:S(2)}) %copy-start.2) | copy-done | bytes 4718616
  180.8 6.6 %shard_map.78 = (bf16[512,1536]{1,0:T(8,128)(2,1)S(1)}, bf16[256,1536]{1,0:T(8,128)(2,1)S(1)}, bf16[256,1536]{1,0:T(8,128)(2,1)S(1)}) custom-call(bf16[512,768]{1,0:T(8,128)(2,1)S(1)} %all_gather.6.a_ref, bf16[512,768]{1,0:T(8,128)(2,1)S(1)} %all_gather.7.b_ref, bf16[1536,1536]{1,0:T(8,128)(2,1)S(1)} %copy-done.2), custom_call_target="tpu_custom_call" | custom-call | flops 2415919104 | bytes 4718592 | tf_op jit(solution)/shard_map/pallas_call | solution.py:108
  187.4 0.1 collective-permute-start.1
  187.5 2.3 %collective-permute-done.1 = bf16[256,1536]{1,0:T(8,128)(2,1)S(1)} collective-permute-done((bf16[256,1536]{1,0:T(8,128)(2,1)S(1)}, bf16[256,1536]{1,0:T(8,128)(2,1)S(1)}, u32[]{:S(2)}, u32[]{:S(2)}) %collective-permute-start.1) | collective-permute-done | bytes 786464 | tf_op jit(solution)/shard_map/ppermute | solution.py:134
  189.8 1.1 add_convert_fusion
  190.9 7.3 %all-to-all-start.2 = ((bf16[16,16,1536]{2,1,0:T(8,128)(2,1)}), bf16[16,16,1536]{2,1,0:T(8,128)(2,1)}, u32[]{:S(2)}, u32[]{:S(2)}) async-start(bf16[16,16,1536]{2,1,0:T(8,128)(2,1)} %bitcast.12), calls=%async_computation.4 | async-start | bytes 1572864 | tf_op jit(solution)/shard_map/all_to_all | solution.py:185
  198.2 0.7 pad_maximum_fusion
  198.9 4.3 %convolution_convert_fusion = bf16[1536,1536]{1,0:T(8,128)(2,1)} fusion(bf16[512,1536]{1,0:T(8,128)(2,1)S(1)} %get-tuple-element.9.normed_ref, bf16[512,1536]{1,0:T(8,128)(2,1)S(1)} %get-tuple-element.12), kind=kOutput, calls=%fused_computation | convolution fusion | flops 2418278400 | bytes 7864320 | tf_op jit(solution)/shard_map/dot_general | solution.py:180
  203.1 7.5 %all-to-all-done.2 = bf16[16,16,1536]{2,1,0:T(8,128)(2,1)} async-done(((bf16[16,16,1536]{2,1,0:T(8,128)(2,1)}), bf16[16,16,1536]{2,1,0:T(8,128)(2,1)}, u32[]{:S(2)}, u32[]{:S(2)}) %all-to-all-start.2) | async-done | bytes 786464 | tf_op jit(solution)/shard_map/all_to_all | solution.py:185
  210.7 1.9 reduce_sum.62
  (8 shorter events, 0.1 us)
Async XLA Ops:
  7.2 78.4 %reduce-scatter.3.cloned.1.call-start = ((), (), s32[]{:S(2)}) async-start(), calls=%async_computation.5 | async-start | bytes 884736 | tf_op jit(solution)/shard_map/reduce_scatter | solution.py:163
  44.8 2.3 %collective-permute-start = (bf16[256,1536]{1,0:T(8,128)(2,1)S(1)}, bf16[256,1536]{1,0:T(8,128)(2,1)S(1)}, u32[]{:S(2)}, u32[]{:S(2)}) collective-permute-start(bf16[256,1536]{1,0:T(8,128)(2,1)S(1)} %bitcast.10), channel_id=1, source_target_pairs={{0,8},{8,0},{1,9},{9,1},{2,10},{10,2},{3,11},{11,3},{4,12},{12,4},... | collective-permute-start | bytes 2359304 | tf_op jit(solution)/shard_map/ppermute | solution.py:134
  47.0 2.3 %copy-start = (bf16[1536,1536]{1,0:T(8,128)(2,1)S(1)}, bf16[1536,1536]{1,0:T(8,128)(2,1)}, u32[]{:S(2)}) copy-start(bf16[1536,1536]{1,0:T(8,128)(2,1)} %w_ref.5) | copy-start | bytes 14155780
  53.1 71.7 %reduce-scatter.5.cloned.1.call-start = ((), (), s32[]{:S(2)}) async-start(), calls=%async_computation.6 | async-start | bytes 884736 | tf_op jit(solution)/shard_map/reduce_scatter | solution.py:164
  53.1 2.3 %copy-start.1 = (bf16[1536,1536]{1,0:T(8,128)(2,1)S(1)}, bf16[1536,1536]{1,0:T(8,128)(2,1)}, u32[]{:S(2)}) copy-start(bf16[1536,1536]{1,0:T(8,128)(2,1)} %w_ref.5) | copy-start | bytes 14155780
  55.5 69.3 %copy-start.3 = (bf16[64,1536]{1,0:T(8,128)(2,1)S(1)}, bf16[64,1536]{1,0:T(8,128)(2,1)}, u32[]{:S(2)}) copy-start(bf16[64,1536]{1,0:T(8,128)(2,1)} %param.9) | copy-start | bytes 589828
  178.5 2.3 %copy-start.2 = (bf16[1536,1536]{1,0:T(8,128)(2,1)S(1)}, bf16[1536,1536]{1,0:T(8,128)(2,1)}, u32[]{:S(2)}) copy-start(bf16[1536,1536]{1,0:T(8,128)(2,1)} %w_ref.5) | copy-start | bytes 14155780
  187.4 2.4 %collective-permute-start.1 = (bf16[256,1536]{1,0:T(8,128)(2,1)S(1)}, bf16[256,1536]{1,0:T(8,128)(2,1)S(1)}, u32[]{:S(2)}, u32[]{:S(2)}) collective-permute-start(bf16[256,1536]{1,0:T(8,128)(2,1)S(1)} %get-tuple-element.11), channel_id=1, source_target_pairs={{0,8},{8,0},{1,9},{9,1},{2,10},{10,2},{3,11},{11,3},{4,12},{12,4},... | collective-permute-start | bytes 2359304 | tf_op jit(solution)/shard_map/ppermute | solution.py:134
  190.9 19.8 %all-to-all-start.2 = ((bf16[16,16,1536]{2,1,0:T(8,128)(2,1)}), bf16[16,16,1536]{2,1,0:T(8,128)(2,1)}, u32[]{:S(2)}, u32[]{:S(2)}) async-start(bf16[16,16,1536]{2,1,0:T(8,128)(2,1)} %bitcast.12), calls=%async_computation.4 | async-start | bytes 1572864 | tf_op jit(solution)/shard_map/all_to_all | solution.py:185
Sparse Core Ops, SparseCore 0:
  53.2 32.3 reduce-scatter.2
  88.3 36.4 reduce-scatter.4
